TPU v7x, 32 devices: a whole 2x2x4 slice. The times are simulated.
32 devices in a mesh: row: 4 (over x, core), col: 8 (over z, y).
Axes of the slice: x: 2, y: 2, z: 4, core: 2. Of those that a mesh axis runs over, the one named last changes fastest.
Arguments:
- pair: bfloat16 [128, 128, 128], P('row', 'col'), may hold values from -6 to 6
- conv_weight: bfloat16 [3, 3, 128, 128], replicated, may hold values from -0.1875 to 0.1875
- conv_bias: float32 [128], replicated, may hold values from -3 to 3
- norm_gain: float32 [128], replicated, may hold values from 0.1 to 1.9
- norm_shift: float32 [128], replicated, may hold values from -2.5 to 2.5
- proj_weight: bfloat16 [128, 512], replicated, may hold values from -0.5 to 0.5
- gate_weight: bfloat16 [128, 128], replicated, may hold values from -0.5 to 0.5
- tri_gain: float32 [128], replicated, may hold values from 0.1 to 1.9
- tri_shift: float32 [128], replicated, may hold values from -2.5 to 2.5
- out_weight: bfloat16 [128, 128], replicated, may hold values from -0.5 to 0.5
Outputs:
- updated: bfloat16 [128, 128, 128], P('row', 'col')
All inputs are finite; a program needn't handle non-finite values.
Results may differ from a plain program's by a relative error of at most 0.0051.
Values may be sent and summed in bfloat16 or wider, within the bound.
A program may use at most 64 MiB of HBM per device.

v0:
```python
import jax
import jax.numpy as jnp
from jax import lax
from jax.sharding import PartitionSpec as P

CH = 128
DILATION_STEP = 2


def with_halo(cells, sides, width):
    for axis, dim in sides:
        count = lax.axis_size(axis)
        ends = count - 1
        head = lax.slice_in_dim(cells, 0, width, axis=dim)
        tail = lax.slice_in_dim(cells, cells.shape[dim] - width, cells.shape[dim], axis=dim)
        cells = jnp.concatenate(
            [
                lax.ppermute(tail, axis, [(i, (i + 1) % count) for i in range(ends)]),
                cells,
                lax.ppermute(head, axis, [((i + 1) % count, i) for i in range(ends)]),
            ],
            axis=dim,
        )
    return cells


def broadcast(value, axis, source):
    kept = jnp.where(lax.axis_index(axis) == source, value, 0).astype(value.dtype)
    return lax.psum(kept, axis)


def layer_norm(values, gain, shift):
    row_mean = jnp.mean(values, -1, keepdims=True)
    centred = values - row_mean
    variance = jnp.mean(centred * centred, -1, keepdims=True)
    return centred * lax.rsqrt(variance + 1e-05) * gain + shift


def on_device(
    pair,
    conv_weight,
    conv_bias,
    norm_gain,
    norm_shift,
    proj_weight,
    gate_weight,
    tri_gain,
    tri_shift,
    out_weight,
):
    row_total, column_total, channels = pair.shape
    padded_pair = with_halo(pair, (("row", 0), ("col", 1)), DILATION_STEP)
    total = pair.astype(jnp.float32) + conv_bias
    for kernel_row in range(3):
        for kernel_column in range(3):
            kernel_window = padded_pair[
                kernel_row * DILATION_STEP : kernel_row * DILATION_STEP + row_total,
                kernel_column * DILATION_STEP : kernel_column * DILATION_STEP + column_total,
                :,
            ]
            product = jnp.dot(
                kernel_window.reshape(row_total * column_total, channels),
                conv_weight[kernel_row, kernel_column],
                preferred_element_type=jnp.float32,
            )
            total = total + product.reshape(row_total, column_total, channels)
    hidden = lax.optimization_barrier(total.astype(jnp.bfloat16))
    normed = layer_norm(hidden.astype(jnp.float32), norm_gain, norm_shift).astype(jnp.bfloat16)
    flat = normed.reshape(row_total * column_total, channels)
    proj = jnp.dot(flat, proj_weight, preferred_element_type=jnp.float32)
    left = (
        (jax.nn.sigmoid(proj[:, :CH]) * proj[:, CH : 2 * CH])
        .astype(jnp.bfloat16)
        .reshape(row_total, column_total, CH)
    )
    right = (
        (jax.nn.sigmoid(proj[:, 2 * CH : 3 * CH]) * proj[:, 3 * CH :])
        .astype(jnp.bfloat16)
        .reshape(row_total, column_total, CH)
    )
    gate = jax.nn.sigmoid(jnp.dot(flat, gate_weight, preferred_element_type=jnp.float32))
    full_rows = lax.all_gather(right, "col", axis=1, tiled=True)
    col_place = lax.axis_index("col")
    row_place = lax.axis_index("row")
    sender = col_place * column_total // row_total
    offset = jnp.clip(col_place * column_total - row_place * row_total, 0, row_total - column_total)
    chosen = lax.dynamic_slice_in_dim(full_rows, offset, column_total, 0)
    right_rows = broadcast(chosen, "row", sender)
    tri = jnp.einsum(
        "ikc,jkc->ijc",
        lax.all_gather(left, "col", axis=1, tiled=True),
        right_rows,
        preferred_element_type=jnp.float32,
    )
    tnorm = (
        layer_norm(tri, tri_gain, tri_shift)
        .astype(jnp.bfloat16)
        .reshape(row_total * column_total, CH)
    )
    update = jnp.dot(tnorm, out_weight, preferred_element_type=jnp.float32)
    result = hidden.astype(jnp.float32).reshape(row_total * column_total, channels) + gate * update
    return result.astype(jnp.bfloat16).reshape(row_total, column_total, channels)


def solution(mesh):
    placed = (P("row", "col", None), P(), P(), P(), P(), P(), P(), P(), P(), P())
    return jax.shard_map(
        on_device, mesh=mesh, in_specs=placed, out_specs=P("row", "col", None), check_vma=False
    )
```

profile of v0, /device:TPU:0, one launch (start us, length us, event | category | flops | bytes accessed | tf_op | source)
XLA Modules:
  0.0 196.6 jit_solution(18442856130691597483)
XLA Ops:
  6.5 0.8 fusion.71
  7.3 2.3 %collective-permute-start = (bf16[2,16,128]{2,1,0:T(8,128)(2,1)S(1)}, bf16[2,16,128]{2,1,0:T(8,128)(2,1)S(1)}, u32[]{:S(2)}, u32[]{:S(2)}) collective-permute-start(bf16[2,16,128]{2,1,0:T(8,128)(2,1)S(1)} %get-tuple-element.10), channel_id=1, source_target_pairs={{0,8},{8,16},{16,24},{1,9},{9,17},{17,25},{2,10},{10,18},{18,26},{... | collective-permute-start | bytes 24584 | tf_op jit(solution)/shard_map/ppermute | solution.py:18
  9.7 1.3 collective-permute-start.1
  11.0 1.1 fusion.47
  12.1 0.9 constant_dynamic-update-slice_fusion.1
  13.0 1.8 collective-permute-done.1
  14.9 1.3 collective-permute-start.3
  16.2 4.5 %collective-permute-start.2 = (bf16[36,2,128]{2,1,0:T(2,128)(2,1)S(1)}, bf16[36,2,128]{2,1,0:T(2,128)(2,1)S(1)}, u32[]{:S(2)}, u32[]{:S(2)}) collective-permute-start(bf16[36,2,128]{2,1,0:T(2,128)(2,1)S(1)} %get-tuple-element.7), channel_id=1, source_target_pairs={{0,1},{1,2},{2,3},{3,4},{4,5},{5,6},{6,7},{8,9},{9,10},{10,11},{11... | collective-permute-start | bytes 55304 | tf_op jit(solution)/shard_map/ppermute | solution.py:18
  20.7 1.1 fusion.21
  21.8 1.1 fusion.25
  22.9 0.9 fusion.35
  23.8 0.9 fusion.41
  24.8 0.9 fusion.32
  25.7 0.9 fusion.39
  26.7 1.1 fusion.10
  27.8 1.0 fusion.12
  29.1 0.2 multiply_reduce_fusion.1
  29.5 0.2 add_convert_fusion.1
  29.7 0.3 fusion.72
  30.1 0.7 copy.38
  30.9 1.3 copy.40
  32.3 42.6 %all-gather.3.cloned.1.call-done = bf16[32,128,128]{2,0,1:T(8,128)(2,1)} async-done(((bf16[32,16,128]{2,0,1:T(8,128)(2,1)}), bf16[32,128,128]{2,0,1:T(8,128)(2,1)}) %all-gather.3.cloned.1.call-update) | async-done | bytes 1048592 | tf_op jit(solution)/shard_map/all_gather | solution.py:82
  74.8 1.4 constant_dynamic-slice_fusion
  76.2 0.7 copy.48
  76.9 0.8 broadcast_select_fusion
  77.8 0.2 fusion.9
  78.1 72.6 %all-gather.5.cloned.1.call-done = bf16[32,128,128]{0,1,2:T(8,128)(2,1)} async-done(((bf16[32,16,128]{0,1,2:T(8,128)(2,1)}), bf16[32,128,128]{0,1,2:T(8,128)(2,1)}) %all-gather.5.cloned.1.call-update) | async-done | bytes 1048592 | tf_op jit(solution)/shard_map/all_gather | solution.py:91
  150.7 33.7 %all-reduce.2.cloned.1.call-done = bf16[16,128,128]{1,0,2:T(8,128)(2,1)} async-done(((bf16[16,128,128]{1,0,2:T(8,128)(2,1)}), bf16[16,128,128]{1,0,2:T(8,128)(2,1)}) %all-reduce.2.cloned.1.call-update) | async-done | bytes 524304 | tf_op jit(solution)/shard_map/psum | solution.py:29
  184.4 3.6 %bitcast_reduce_fusion = (f32[32,16]{0,1:T(8,128)S(1)}, f32[128,16,32]{2,1,0:T(8,128)S(1)}) fusion(bf16[16,128,128]{1,0,2:T(8,128)(2,1)} %all-reduce.2.cloned.1.call-done, bf16[32,128,128]{0,1,2:T(8,128)(2,1)} %all-gather.5.cloned.1.call-done), kind=kOutput, calls=%fused_computation.17 | convolution fusion | flops 16842240 | bytes 1837056 | tf_op jit(solution)/shard_map/ikc,jkc->ijc/dot_general | solution.py:89
  188.0 0.5 copy.41
  188.6 0.2 multiply_reduce_fusion
  189.2 0.8 fusion.11
  (40 shorter events, 1.3 us)
Async XLA Ops:
  6.5 23.2 %copy-start = (bf16[128,512]{1,0:T(8,128)(2,1)S(1)}, bf16[128,512]{1,0:T(8,128)(2,1)}, u32[]{:S(2)}) copy-start(bf16[128,512]{1,0:T(8,128)(2,1)} %param.15) | copy-start | bytes 393220
  6.5 22.9 %copy-start.3 = (f32[128]{0:T(128)S(1)}, f32[128]{0:T(128)}, u32[]{:S(2)}) copy-start(f32[128]{0:T(128)} %param.13) | copy-start | bytes 1540
  6.5 22.9 %copy-start.2 = (f32[128]{0:T(128)S(1)}, f32[128]{0:T(128)}, u32[]{:S(2)}) copy-start(f32[128]{0:T(128)} %param.14) | copy-start | bytes 1540
  6.5 68.3 %all-gather.3.cloned.1.call-start = ((), (), s32[]{:S(2)}) async-start(), calls=%async_computation | async-start | bytes 1179648 | tf_op jit(solution)/shard_map/all_gather | solution.py:82
  7.3 4.7 %collective-permute-start = (bf16[2,16,128]{2,1,0:T(8,128)(2,1)S(1)}, bf16[2,16,128]{2,1,0:T(8,128)(2,1)S(1)}, u32[]{:S(2)}, u32[]{:S(2)}) collective-permute-start(bf16[2,16,128]{2,1,0:T(8,128)(2,1)S(1)} %get-tuple-element.10), channel_id=1, source_target_pairs={{0,8},{8,16},{16,24},{1,9},{9,17},{17,25},{2,10},{10,18},{18,26},{... | collective-permute-start | bytes 24584 | tf_op jit(solution)/shard_map/ppermute | solution.py:18
  9.7 5.2 %collective-permute-start.1 = (bf16[2,16,128]{2,1,0:T(8,128)(2,1)S(1)}, bf16[2,16,128]{2,1,0:T(8,128)(2,1)S(1)}, u32[]{:S(2)}, u32[]{:S(2)}) collective-permute-start(bf16[2,16,128]{2,1,0:T(8,128)(2,1)S(1)} %get-tuple-element.9), channel_id=1, source_target_pairs={{8,0},{16,8},{24,16},{9,1},{17,9},{25,17},{10,2},{18,10},{26,18},{... | collective-permute-start | bytes 24584 | tf_op jit(solution)/shard_map/ppermute | solution.py:20
  14.9 9.9 %collective-permute-start.3 = (bf16[36,2,128]{2,1,0:T(2,128)(2,1)S(1)}, bf16[36,2,128]{2,1,0:T(2,128)(2,1)S(1)}, u32[]{:S(2)}, u32[]{:S(2)}) collective-permute-start(bf16[36,2,128]{2,1,0:T(2,128)(2,1)S(1)} %get-tuple-element.8), channel_id=1, source_target_pairs={{1,0},{2,1},{3,2},{4,3},{5,4},{6,5},{7,6},{9,8},{10,9},{11,10},{12... | collective-permute-start | bytes 55304 | tf_op jit(solution)/shard_map/ppermute | solution.py:20
  16.2 6.7 %collective-permute-start.2 = (bf16[36,2,128]{2,1,0:T(2,128)(2,1)S(1)}, bf16[36,2,128]{2,1,0:T(2,128)(2,1)S(1)}, u32[]{:S(2)}, u32[]{:S(2)}) collective-permute-start(bf16[36,2,128]{2,1,0:T(2,128)(2,1)S(1)} %get-tuple-element.7), channel_id=1, source_target_pairs={{0,1},{1,2},{2,3},{3,4},{4,5},{5,6},{6,7},{8,9},{9,10},{10,11},{11... | collective-permute-start | bytes 55304 | tf_op jit(solution)/shard_map/ppermute | solution.py:18
  29.1 48.8 %copy-start.6 = (bf16[128,128]{1,0:T(8,128)(2,1)S(1)}, bf16[128,128]{1,0:T(8,128)(2,1)}, u32[]{:S(2)}) copy-start(bf16[128,128]{1,0:T(8,128)(2,1)} %param.16) | copy-start | bytes 98308
  30.9 119.8 %all-gather.5.cloned.1.call-start = ((), (), s32[]{:S(2)}) async-start(), calls=%async_computation.2 | async-start | bytes 4718592 | tf_op jit(solution)/shard_map/all_gather | solution.py:91
  32.2 152.2 %all-reduce.2.cloned.1.call-start = ((), (), s32[]{:S(2)}) async-start(), calls=%async_computation.1 | async-start | bytes 1048576 | tf_op jit(solution)/shard_map/psum | solution.py:29
  77.8 111.2 %copy-start.4 = (f32[128]{0:T(128)S(1)}, f32[128]{0:T(128)}, u32[]{:S(2)}) copy-start(f32[128]{0:T(128)} %param.18) | copy-start | bytes 1540
  77.8 111.1 %copy-start.5 = (f32[128]{0:T(128)S(1)}, f32[128]{0:T(128)}, u32[]{:S(2)}) copy-start(f32[128]{0:T(128)} %param.17) | copy-start | bytes 1540
  78.1 111.1 %copy-start.1 = (bf16[128,128]{1,0:T(8,128)(2,1)S(1)}, bf16[128,128]{1,0:T(8,128)(2,1)}, u32[]{:S(2)}) copy-start(bf16[128,128]{1,0:T(8,128)(2,1)} %param.19) | copy-start | bytes 98308
Sparse Core Ops, SparseCore 0:
  31.0 43.8 all-gather.2
  76.9 73.7 all-gather.4
  153.0 31.3 all-reduce.1
where the time goes:
time: 197 us
  waiting for transfers between devices  151 us (77%)
  matrix products  13.9 us (7%)
  between operations  13.4 us (7%)
  starting transfers between devices  9.56 us (5%)
  local copies, waits for them, and re-layouts  6.8 us (3%)
  other arithmetic  2.06 us (1%)
    all_gather x1, waiting for transfers between devices, on_device(): lax.all_gather(left, 'col', axis=1, tiled=True)  72.6 us
    all_gather x1, waiting for transfers between devices, on_device(): full_rows = lax.all_gather(right, 'col', axis=1, tiled=True)  42.6 us
    psum x1, waiting for transfers between devices, broadcast(): return lax.psum(kept, axis)  33.7 us
    dot_general x9, matrix products, on_device(): jnp.dot(kernel_window.reshape(row_total * column_total, channels), conv_w...  9.04 us
    ppermute x2, starting transfers between devices, with_halo(): lax.ppermute(tail, axis, [(i, (i + 1) % count) for i in range(ends)])  6.89 us
  transfers between devices with their start and end apart: 7, of which 4 were waited for; matrix products, arithmetic and copies ran while one was open for 5% of the time, Pallas kernels for 0%

commit v1 on v0

v1 whole, which is shorter than its diff:
```python
import functools

import jax
import jax.numpy as jnp
from jax import lax
from jax.experimental import pallas as pl
from jax.experimental.pallas import tpu as pltpu
from jax.sharding import PartitionSpec as P

STEP = 2
EDGE = 8
SIDES = ((-1, 0), (1, 0), (0, -1), (0, 1), (-1, -1), (-1, 1), (1, -1), (1, 1))
F32, BF16 = jnp.float32, jnp.bfloat16


def layer_norm(values, gain, shift):
    row_mean = jnp.mean(values, -1, keepdims=True)
    centred = values - row_mean
    variance = jnp.mean(centred * centred, -1, keepdims=True)
    return centred * lax.rsqrt(variance + 1e-05) * gain + shift


def swap_blocks(parts, width):
    count = len(parts)
    parts = list(parts)
    lane = lax.broadcasted_iota(jnp.int32, parts[0].shape, 1)
    bit = 1
    while bit < count:
        low = (lane & (bit * width)) == 0
        for p in range(count):
            if p & bit == 0:
                a, b = parts[p], parts[p + bit]
                parts[p] = jnp.where(low, a, pltpu.roll(b, bit * width, 1))
                parts[p + bit] = jnp.where(low, pltpu.roll(a, 128 - bit * width, 1), b)
        bit *= 2
    return parts


def kernel(
    sizes,
    pair, conv_w, conv_b, n_gain, n_shift, proj_w, gate_w, t_gain, t_shift, out_w,
    out,
    padded, strips, halo_row, halo_col, halo_cor, hidden, gate,
    send_l, send_r, all_l, all_r, left32, acc, send_t, all_t, update,
    halo_s, halo_r, l_s, l_r, r_s, r_r, g_s, g_r, t_s, t_r,
):
    n_row, n, rows, cols = sizes
    group = rows // n
    width = 128 // n
    flat = rows * cols
    half = rows // 2
    r, c = lax.axis_index("row"), lax.axis_index("col")

    def exists(dr, dc):
        ok = None
        if dr:
            ok = (r + dr >= 0) & (r + dr < n_row)
        if dc:
            col_ok = (c + dc >= 0) & (c + dc < n)
            ok = col_ok if ok is None else ok & col_ok
        return ok

    barrier = pltpu.get_barrier_semaphore()
    for k in range(1, n):
        pl.semaphore_signal(barrier, inc=1, device_id=(r, lax.rem(c + k, n)), device_id_type=pl.DeviceIdType.MESH)
    for k in range(1, n_row):
        pl.semaphore_signal(barrier, inc=1, device_id=(lax.rem(r + k, n_row), c), device_id_type=pl.DeviceIdType.MESH)
    for dr, dc in SIDES[4:]:
        @pl.when(exists(dr, dc))
        def _():
            pl.semaphore_signal(barrier, inc=1, device_id=(r + dr, c + dc), device_id_type=pl.DeviceIdType.MESH)

    padded[...] = jnp.zeros_like(padded)
    padded[STEP : STEP + rows, EDGE : EDGE + cols, :] = pair[...].astype(F32)
    for at, col in enumerate((0, 1, cols - 2, cols - 1)):
        strips[at] = padded[STEP : STEP + rows, EDGE + col, :].astype(BF16)

    beside_r = (r > 0).astype(jnp.int32) + (r < n_row - 1).astype(jnp.int32)
    beside_c = (c > 0).astype(jnp.int32) + (c < n - 1).astype(jnp.int32)
    pl.semaphore_wait(barrier, n - 1 + n_row - 1 + beside_r * beside_c)

    def halo_copy(at, dr, dc):
        if dc == 0:
            src = pair.at[pl.ds(0 if dr < 0 else rows - STEP, STEP)]
            dst = halo_row.at[1 if dr < 0 else 0]
        else:
            src = strips.at[pl.ds(0 if dc < 0 else 2, 2)]
            if dr == 0:
                dst = halo_col.at[1 if dc < 0 else 0]
            else:
                src = strips.at[pl.ds(0 if dc < 0 else 2, 2), pl.ds(0 if dr < 0 else rows - 16, 16)]
                dst = halo_cor.at[at - 4]
        return pltpu.make_async_remote_copy(
            src_ref=src, dst_ref=dst, send_sem=halo_s.at[at], recv_sem=halo_r.at[at],
            device_id=(r + dr, c + dc), device_id_type=pl.DeviceIdType.MESH,
        )

    for at, (dr, dc) in enumerate(SIDES):
        @pl.when(exists(dr, dc))
        def _():
            halo_copy(at, dr, dc).start()

    for at, (dr, dc) in enumerate(SIDES):
        @pl.when(exists(-dr, -dc))
        def _():
            halo_copy(at, dr, dc).wait_recv()
            first_row = 0 if dr > 0 else STEP + rows
            first_col = EDGE - 2 if dc > 0 else EDGE + cols
            if dc == 0:
                padded[first_row : first_row + STEP, EDGE : EDGE + cols, :] = halo_row[1 if dr < 0 else 0].astype(F32)
            elif dr == 0:
                got = halo_col[1 if dc < 0 else 0].astype(F32)
                for j in range(2):
                    padded[STEP : STEP + rows, first_col + j, :] = got[j]
            else:
                got = halo_cor[at - 4].astype(F32)
                part = slice(0, 2) if dr < 0 else slice(14, 16)
                for j in range(2):
                    padded[first_row : first_row + STEP, first_col + j, :] = got[j, part]

    shifted = [
        padded[:, EDGE + STEP * b : EDGE + STEP * b + cols, :].astype(BF16) for b in (-1, 0, 1)
    ]
    wide = jnp.concatenate(shifted, axis=2)
    total = pair[...].astype(F32).reshape(flat, 128) + conv_b[...]
    for a in range(3):
        total = total + jnp.dot(
            wide[a * STEP : a * STEP + rows].reshape(flat, 3 * 128), conv_w[a],
            preferred_element_type=F32,
        )
    rounded = total.astype(BF16)
    hidden[...] = rounded
    normed = layer_norm(rounded.astype(F32), n_gain[...], n_shift[...]).astype(BF16)

    def gated(first):
        part = jnp.dot(normed, proj_w[:, first : first + 256], preferred_element_type=F32)
        return jax.nn.sigmoid(part[:, :128]) * part[:, 128:]

    step = group * cols

    def scatter(values, sent, whole):
        packed = swap_blocks([values[p * step : (p + 1) * step] for p in range(n)], width)
        for p in range(n):
            sent[p] = packed[p].astype(BF16).reshape(group, cols, 128)

    def block_copy(k, sent, whole, s_sem, r_sem):
        to = lax.rem(c + k, n)
        return pltpu.make_async_remote_copy(
            src_ref=sent.at[to], dst_ref=whole.at[c], send_sem=s_sem.at[k], recv_sem=r_sem.at[k],
            device_id=(r, to), device_id_type=pl.DeviceIdType.MESH,
        )

    mine_r = all_r.at[r]
    scatter(gated(256), send_r, mine_r)
    for k in range(1, n):
        block_copy(k, send_r, mine_r, r_s, r_r).start()
    scatter(gated(0), send_l, all_l)
    for k in range(1, n):
        block_copy(k, send_l, all_l, l_s, l_r).start()
    all_r[r, c] = send_r[c]
    all_l[c] = send_l[c]
    gate[...] = jax.nn.sigmoid(jnp.dot(normed, gate_w[...], preferred_element_type=F32))

    for k in range(1, n):
        block_copy(k, send_r, mine_r, r_s, r_r).wait_recv()

    def row_copy(k):
        to = lax.rem(r + k, n_row)
        return pltpu.make_async_remote_copy(
            src_ref=all_r.at[r], dst_ref=all_r.at[r], send_sem=g_s.at[k], recv_sem=g_r.at[k],
            device_id=(to, c), device_id_type=pl.DeviceIdType.MESH,
        )

    for k in range(1, n_row):
        row_copy(k).start()
    for k in range(1, n):
        block_copy(k, send_l, all_l, l_s, l_r).wait_recv()
    for g in range(group):
        left32[g] = all_l[:, g].reshape(n * cols, 128).astype(F32)

    lane_block = lax.broadcasted_iota(jnp.int32, (half, 128), 1) // width
    turn = lax.broadcasted_iota(jnp.int32, (half, 128), 0) // group
    first_half = ((lane_block - turn + n) & (n - 1)) < n // 2

    def back_copy(to, at):
        return pltpu.make_async_remote_copy(
            src_ref=send_t.at[to], dst_ref=all_t.at[c], send_sem=t_s.at[to], recv_sem=t_r.at[at],
            device_id=(r, to), device_id_type=pl.DeviceIdType.MESH,
        )

    def one_row_block(s, _):
        rp = lax.rem(r - s + n_row, n_row)

        @pl.when(s > 0)
        def _():
            pltpu.make_async_remote_copy(
                src_ref=all_r.at[rp], dst_ref=all_r.at[rp], send_sem=g_s.at[s], recv_sem=g_r.at[s],
                device_id=(rp, c), device_id_type=pl.DeviceIdType.MESH,
            ).wait_recv()

        def one_group(gj, _):
            right = all_r[rp, :, gj].reshape(n * cols, 128).astype(F32)
            for rho in range(n):
                turned = pltpu.roll(right, rho * width, 1) if rho else right
                for gi in range(group):
                    acc[gi, pl.ds(rho * group + gj, 1), :] = jnp.sum(
                        left32[gi] * turned, axis=0, keepdims=True
                    )
            return 0

        lax.fori_loop(0, group, one_group, 0)
        for gi in range(group):
            low, high = acc[gi, :half], acc[gi, half:]
            send_t[2 * rp, gi] = jnp.where(first_half, low, high).astype(BF16)
            send_t[2 * rp + 1, gi] = jnp.where(first_half, high, low).astype(BF16)
        for h in range(2):
            to = 2 * rp + h

            @pl.when(to != c)
            def _():
                back_copy(to, c).start()

            @pl.when(to == c)
            def _():
                all_t[c] = send_t[c]

        return 0

    lax.fori_loop(0, n_row, one_row_block, 0)

    for k in range(1, n):
        at = lax.rem(c + k, n)
        back_copy(at, at).wait_recv()
    parts = swap_blocks([all_t[p].astype(F32).reshape(group * half, 128) for p in range(n)], width)
    tri = jnp.concatenate(parts, axis=0)
    tnorm = layer_norm(tri, t_gain[...], t_shift[...]).astype(BF16)
    moved = jnp.dot(tnorm, out_w[...], preferred_element_type=F32)
    for b in range(n):
        for gi in range(group):
            for rho in range(n // 2):
                at = (b * group + gi) * half + rho * group
                j = ((b - rho) % (n // 2)) * group
                update[b * group + gi, j : j + group, :] = moved[at : at + group]
    result = hidden[...].astype(F32) + gate[...] * update[...].reshape(flat, 128)
    out[...] = result.astype(BF16).reshape(rows, cols, 128)

    for at, (dr, dc) in enumerate(SIDES):
        @pl.when(exists(dr, dc))
        def _():
            halo_copy(at, dr, dc).wait_send()
    for k in range(1, n):
        block_copy(k, send_r, mine_r, r_s, r_r).wait_send()
        block_copy(k, send_l, all_l, l_s, l_r).wait_send()
        back_copy(lax.rem(c + k, n), c).wait_send()
    for k in range(1, n_row):
        row_copy(k).wait_send()


def on_device(n_row, n, pair, conv_weight, conv_bias, norm_gain, norm_shift, proj_weight,
              gate_weight, tri_gain, tri_shift, out_weight):
    rows, cols, channels = pair.shape
    group = rows // n
    flat = rows * cols
    dma = pltpu.SemaphoreType.DMA
    flat_vec = lambda v: v.reshape(1, 128)
    return pl.pallas_call(
        functools.partial(kernel, (n_row, n, rows, cols)),
        out_shape=jax.ShapeDtypeStruct(pair.shape, BF16),
        in_specs=[pl.BlockSpec(memory_space=pltpu.VMEM)] * 10,
        out_specs=pl.BlockSpec(memory_space=pltpu.VMEM),
        scratch_shapes=[
            pltpu.VMEM((rows + 2 * STEP, EDGE + cols + 8, 128), F32),
            pltpu.VMEM((4, rows, 128), BF16),
            pltpu.VMEM((2, STEP, cols, 128), BF16),
            pltpu.VMEM((2, 2, rows, 128), BF16),
            pltpu.VMEM((4, 2, 16, 128), BF16),
            pltpu.VMEM((flat, 128), BF16),
            pltpu.VMEM((flat, 128), F32),
            pltpu.VMEM((n, group, cols, 128), BF16),
            pltpu.VMEM((n, group, cols, 128), BF16),
            pltpu.VMEM((n, group, cols, 128), BF16),
            pltpu.VMEM((n_row, n, group, cols, 128), BF16),
            pltpu.VMEM((group, n * cols, 128), F32),
            pltpu.VMEM((group, rows, 128), F32),
            pltpu.VMEM((n, group, rows // 2, 128), BF16),
            pltpu.VMEM((n, group, rows // 2, 128), BF16),
            pltpu.VMEM((rows, cols, 128), F32),
            dma((8,)), dma((8,)), dma((n,)), dma((n,)), dma((n,)), dma((n,)),
            dma((n_row,)), dma((n_row,)), dma((n,)), dma((n,)),
        ],
        compiler_params=pltpu.CompilerParams(
            collective_id=0, has_side_effects=True, vmem_limit_bytes=48 * 1024 * 1024
        ),
    )(
        pair, conv_weight.reshape(3, 3 * 128, 128), flat_vec(conv_bias), flat_vec(norm_gain),
        flat_vec(norm_shift), proj_weight, gate_weight, flat_vec(tri_gain), flat_vec(tri_shift),
        out_weight,
    )


def solution(mesh):
    placed = (P("row", "col", None),) + (P(),) * 9
    return jax.shard_map(
        functools.partial(on_device, mesh.shape["row"], mesh.shape["col"]),
        mesh=mesh, in_specs=placed, out_specs=P("row", "col", None), check_vma=False,
    )
```

time: 197 us -> 33.9 us (0.17)
  the two profiles are of different devices: /device:TPU:0 before, /device:TPU:3 now
where the time goes in v1:
time: 33.9 us; the launch traced here: 33.6 us
  Pallas kernels  27.9 us (82%)
  local copies, waits for them, and re-layouts  5.64 us (17%)
    pallas_call x1, Pallas kernels, on_device(): pl.pallas_call(functools.partial(kernel, (n_row, n, rows, cols)), out_sha...  27.9 us
    unnamed x21, local copies, waits for them, and re-layouts  5.64 us

profile of v1, /device:TPU:3, one launch (start us, length us, event | category | flops | bytes accessed | tf_op | source)
XLA Modules:
  0.0 33.6 jit_solution(17520706927161203170)
XLA Ops:
  0.0 0.0 copy-start.8
  0.0 0.0 copy-start.9
  0.0 0.0 copy-start.5
  0.0 0.0 copy-start.6
  0.0 0.0 copy-start.7
  0.0 0.6 %copy-done.8 = f32[128]{0:T(128)S(1)} copy-done((f32[128]{0:T(128)S(1)}, f32[128]{0:T(128)}, u32[]{:S(2)}) %copy-start.8) | copy-done | bytes 536
  0.7 0.0 copy-done.9
  0.7 0.0 copy-done.5
  0.7 0.0 copy-done.6
  0.7 0.0 copy-done.7
  0.7 0.0 copy-start
  0.7 1.0 %copy-done = bf16[3,3,128,128]{3,2,1,0:T(8,128)(2,1)S(1)} copy-done((bf16[3,3,128,128]{3,2,1,0:T(8,128)(2,1)S(1)}, bf16[3,3,128,128]{3,2,1,0:T(8,128)(2,1)}, u32[]{:S(2)}) %copy-start) | copy-done | bytes 294936
  1.7 0.0 copy-start.1
  1.7 0.9 %copy-done.1 = bf16[32,16,128]{2,1,0:T(8,128)(2,1)S(1)} copy-done((bf16[32,16,128]{2,1,0:T(8,128)(2,1)S(1)}, bf16[32,16,128]{2,1,0:T(8,128)(2,1)}, u32[]{:S(2)}) %copy-start.1) | copy-done | bytes 131096
  2.6 0.0 copy-start.2
  2.6 0.9 %copy-done.2 = bf16[128,512]{1,0:T(8,128)(2,1)S(1)} copy-done((bf16[128,512]{1,0:T(8,128)(2,1)S(1)}, bf16[128,512]{1,0:T(8,128)(2,1)}, u32[]{:S(2)}) %copy-start.2) | copy-done | bytes 131096
  3.5 0.0 copy-start.3
  3.5 0.8 %copy-done.3 = bf16[128,128]{1,0:T(8,128)(2,1)S(1)} copy-done((bf16[128,128]{1,0:T(8,128)(2,1)S(1)}, bf16[128,128]{1,0:T(8,128)(2,1)}, u32[]{:S(2)}) %copy-start.3) | copy-done | bytes 32792
  4.2 0.0 copy-start.4
  4.3 0.8 %copy-done.4 = bf16[128,128]{1,0:T(8,128)(2,1)S(1)} copy-done((bf16[128,128]{1,0:T(8,128)(2,1)S(1)}, bf16[128,128]{1,0:T(8,128)(2,1)}, u32[]{:S(2)}) %copy-start.4) | copy-done | bytes 32792
  5.0 27.9 %shard_map.100 = bf16[32,16,128]{2,1,0:T(8,128)(2,1)S(1)} custom-call(bf16[32,16,128]{2,1,0:T(8,128)(2,1)S(1)} %copy-done.1, bf16[3,384,128]{2,1,0:T(8,128)(2,1)S(1)} %bitcast.6, f32[1,128]{1,0:T(1,128)S(1)} %bitcast.7, f32[1,128]{1,0:T(1,128)S(1)} %bitcast.8, f32[1,128]{1,0:T(1,128)S(1)} %bitcast.9, bf16[128,512]{1,0:T(8,128)(2,1)S(1)} %copy-done.2, ...), custom_call_target="tpu_custom_call" | custom-call | tf_op jit(solution)/shard_map/pallas_call | solution.py:266
  32.9 0.7 %copy.12 = bf16[32,16,128]{2,1,0:T(8,128)(2,1)} copy(bf16[32,16,128]{2,1,0:T(8,128)(2,1)S(1)} %shard_map.100) | data formatting | bytes 262144
Async XLA Ops:
  0.0 0.7 %copy-start.8 = (f32[128]{0:T(128)S(1)}, f32[128]{0:T(128)}, u32[]{:S(2)}) copy-start(f32[128]{0:T(128)} %param.17) | copy-start | bytes 1540
  0.0 0.7 %copy-start.9 = (f32[128]{0:T(128)S(1)}, f32[128]{0:T(128)}, u32[]{:S(2)}) copy-start(f32[128]{0:T(128)} %param.18) | copy-start | bytes 1540
  0.0 0.7 %copy-start.5 = (f32[128]{0:T(128)S(1)}, f32[128]{0:T(128)}, u32[]{:S(2)}) copy-start(f32[128]{0:T(128)} %param.12) | copy-start | bytes 1540
  0.0 0.7 %copy-start.6 = (f32[128]{0:T(128)S(1)}, f32[128]{0:T(128)}, u32[]{:S(2)}) copy-start(f32[128]{0:T(128)} %param.13) | copy-start | bytes 1540
  0.0 0.7 %copy-start.7 = (f32[128]{0:T(128)S(1)}, f32[128]{0:T(128)}, u32[]{:S(2)}) copy-start(f32[128]{0:T(128)} %param.14) | copy-start | bytes 1540
  0.7 1.0 %copy-start = (bf16[3,3,128,128]{3,2,1,0:T(8,128)(2,1)S(1)}, bf16[3,3,128,128]{3,2,1,0:T(8,128)(2,1)}, u32[]{:S(2)}) copy-start(bf16[3,3,128,128]{3,2,1,0:T(8,128)(2,1)} %param.11) | copy-start | bytes 884740
  1.7 0.9 %copy-start.1 = (bf16[32,16,128]{2,1,0:T(8,128)(2,1)S(1)}, bf16[32,16,128]{2,1,0:T(8,128)(2,1)}, u32[]{:S(2)}) copy-start(bf16[32,16,128]{2,1,0:T(8,128)(2,1)} %pair.1) | copy-start | bytes 393220
  2.6 0.9 %copy-start.2 = (bf16[128,512]{1,0:T(8,128)(2,1)S(1)}, bf16[128,512]{1,0:T(8,128)(2,1)}, u32[]{:S(2)}) copy-start(bf16[128,512]{1,0:T(8,128)(2,1)} %proj_w.1) | copy-start | bytes 393220
  3.5 0.8 %copy-start.3 = (bf16[128,128]{1,0:T(8,128)(2,1)S(1)}, bf16[128,128]{1,0:T(8,128)(2,1)}, u32[]{:S(2)}) copy-start(bf16[128,128]{1,0:T(8,128)(2,1)} %gate_w.1) | copy-start | bytes 98308
  4.2 0.8 %copy-start.4 = (bf16[128,128]{1,0:T(8,128)(2,1)S(1)}, bf16[128,128]{1,0:T(8,128)(2,1)}, u32[]{:S(2)}) copy-start(bf16[128,128]{1,0:T(8,128)(2,1)} %out_w.1) | copy-start | bytes 98308

commit v2 on v1

--- a/solution.py
+++ b/solution.py
@@ -38,11 +38,12 @@
 
 def kernel(
     sizes,
+    pair_in, conv_w_in, conv_b_in, n_gain_in, n_shift_in, proj_w_in, gate_w_in, t_gain_in, t_shift_in, out_w_in,
+    out,
     pair, conv_w, conv_b, n_gain, n_shift, proj_w, gate_w, t_gain, t_shift, out_w,
-    out,
     padded, strips, halo_row, halo_col, halo_cor, hidden, gate,
     send_l, send_r, all_l, all_r, left32, acc, send_t, all_t, update,
-    halo_s, halo_r, l_s, l_r, r_s, r_r, g_s, g_r, t_s, t_r,
+    in_s, halo_s, halo_r, l_s, l_r, r_s, r_r, x_s, x_r, g_s, g_r, t_s, t_r,
 ):
     n_row, n, rows, cols = sizes
     group = rows // n
@@ -50,6 +51,17 @@
     flat = rows * cols
     half = rows // 2
     r, c = lax.axis_index("row"), lax.axis_index("col")
+
+    loads = [
+        pltpu.make_async_copy(src, dst, in_s.at[at])
+        for at, (src, dst) in enumerate((
+            (pair_in, pair), (conv_w_in, conv_w), (conv_b_in, conv_b), (n_gain_in, n_gain),
+            (n_shift_in, n_shift), (proj_w_in, proj_w), (gate_w_in, gate_w), (t_gain_in, t_gain),
+            (t_shift_in, t_shift), (out_w_in, out_w),
+        ))
+    ]
+    for load in loads:
+        load.start()
 
     def exists(dr, dc):
         ok = None
@@ -71,6 +83,7 @@
             pl.semaphore_signal(barrier, inc=1, device_id=(r + dr, c + dc), device_id_type=pl.DeviceIdType.MESH)
 
     padded[...] = jnp.zeros_like(padded)
+    loads[0].wait()
     padded[STEP : STEP + rows, EDGE : EDGE + cols, :] = pair[...].astype(F32)
     for at, col in enumerate((0, 1, cols - 2, cols - 1)):
         strips[at] = padded[STEP : STEP + rows, EDGE + col, :].astype(BF16)
@@ -100,6 +113,8 @@
         def _():
             halo_copy(at, dr, dc).start()
 
+    for load in loads[1:]:
+        load.wait()
     for at, (dr, dc) in enumerate(SIDES):
         @pl.when(exists(-dr, -dc))
         def _():
@@ -138,7 +153,7 @@
 
     step = group * cols
 
-    def scatter(values, sent, whole):
+    def scatter(values, sent):
         packed = swap_blocks([values[p * step : (p + 1) * step] for p in range(n)], width)
         for p in range(n):
             sent[p] = packed[p].astype(BF16).reshape(group, cols, 128)
@@ -150,29 +165,45 @@
             device_id=(r, to), device_id_type=pl.DeviceIdType.MESH,
         )
 
+    n_chip = n_row // 2
+    chip, core = r // 2, lax.rem(r, 2)
+    beside = chip * 2 + 1 - core
+
+    def row_of(s):
+        return lax.rem(chip - s // 2 + n_chip, n_chip) * 2 + lax.rem(core + s, 2)
+
+    def chip_copy(m, at):
+        return pltpu.make_async_remote_copy(
+            src_ref=all_r.at[r, at], dst_ref=all_r.at[r, at],
+            send_sem=x_s.at[m, at], recv_sem=x_r.at[m, at],
+            device_id=(lax.rem(chip + m, n_chip) * 2 + core, c), device_id_type=pl.DeviceIdType.MESH,
+        )
+
+    def core_copy(s):
+        row = row_of(s)
+        return pltpu.make_async_remote_copy(
+            src_ref=all_r.at[row], dst_ref=all_r.at[row],
+            send_sem=g_s.at[s], recv_sem=g_r.at[s],
+            device_id=(beside, c), device_id_type=pl.DeviceIdType.MESH,
+        )
+
     mine_r = all_r.at[r]
-    scatter(gated(256), send_r, mine_r)
+    scatter(gated(256), send_r)
     for k in range(1, n):
         block_copy(k, send_r, mine_r, r_s, r_r).start()
-    scatter(gated(0), send_l, all_l)
+    all_r[r, c] = send_r[c]
+    for m in range(1, n_chip):
+        chip_copy(m, c).start()
+    scatter(gated(0), send_l)
     for k in range(1, n):
         block_copy(k, send_l, all_l, l_s, l_r).start()
-    all_r[r, c] = send_r[c]
     all_l[c] = send_l[c]
+    for k in range(1, n):
+        block_copy(k, send_r, mine_r, r_s, r_r).wait_recv()
+        for m in range(1, n_chip):
+            chip_copy(m, lax.rem(c + n - k, n)).start()
+    core_copy(0).start()
     gate[...] = jax.nn.sigmoid(jnp.dot(normed, gate_w[...], preferred_element_type=F32))
-
-    for k in range(1, n):
-        block_copy(k, send_r, mine_r, r_s, r_r).wait_recv()
-
-    def row_copy(k):
-        to = lax.rem(r + k, n_row)
-        return pltpu.make_async_remote_copy(
-            src_ref=all_r.at[r], dst_ref=all_r.at[r], send_sem=g_s.at[k], recv_sem=g_r.at[k],
-            device_id=(to, c), device_id_type=pl.DeviceIdType.MESH,
-        )
-
-    for k in range(1, n_row):
-        row_copy(k).start()
     for k in range(1, n):
         block_copy(k, send_l, all_l, l_s, l_r).wait_recv()
     for g in range(group):
@@ -189,13 +220,25 @@
         )
 
     def one_row_block(s, _):
-        rp = lax.rem(r - s + n_row, n_row)
-
-        @pl.when(s > 0)
+        rp = row_of(s)
+        even = lax.rem(s, 2) == 0
+
+        @pl.when(even & (s > 0))
+        def _():
+            for at in range(n):
+                pltpu.make_async_remote_copy(
+                    src_ref=all_r.at[rp, at], dst_ref=all_r.at[rp, at],
+                    send_sem=x_s.at[s // 2, at], recv_sem=x_r.at[s // 2, at],
+                    device_id=(rp, c), device_id_type=pl.DeviceIdType.MESH,
+                ).wait_recv()
+            core_copy(s).start()
+
+        @pl.when(jnp.logical_not(even))
         def _():
             pltpu.make_async_remote_copy(
-                src_ref=all_r.at[rp], dst_ref=all_r.at[rp], send_sem=g_s.at[s], recv_sem=g_r.at[s],
-                device_id=(rp, c), device_id_type=pl.DeviceIdType.MESH,
+                src_ref=all_r.at[rp], dst_ref=all_r.at[rp],
+                send_sem=g_s.at[s - 1], recv_sem=g_r.at[s - 1],
+                device_id=(beside, c), device_id_type=pl.DeviceIdType.MESH,
             ).wait_recv()
 
         def one_group(gj, _):
@@ -252,8 +295,11 @@
         block_copy(k, send_r, mine_r, r_s, r_r).wait_send()
         block_copy(k, send_l, all_l, l_s, l_r).wait_send()
         back_copy(lax.rem(c + k, n), c).wait_send()
-    for k in range(1, n_row):
-        row_copy(k).wait_send()
+    for m in range(n_chip):
+        core_copy(2 * m).wait_send()
+        for at in range(n):
+            if m:
+                chip_copy(m, at).wait_send()
 
 
 def on_device(n_row, n, pair, conv_weight, conv_bias, norm_gain, norm_shift, proj_weight,
@@ -266,9 +312,16 @@
     return pl.pallas_call(
         functools.partial(kernel, (n_row, n, rows, cols)),
         out_shape=jax.ShapeDtypeStruct(pair.shape, BF16),
-        in_specs=[pl.BlockSpec(memory_space=pltpu.VMEM)] * 10,
+        in_specs=[pl.BlockSpec(memory_space=pltpu.HBM)] * 10,
         out_specs=pl.BlockSpec(memory_space=pltpu.VMEM),
         scratch_shapes=[
+            pltpu.VMEM((rows, cols, 128), BF16),
+            pltpu.VMEM((3, 3 * 128, 128), BF16),
+            *[pltpu.VMEM((1, 128), F32)] * 3,
+            pltpu.VMEM((128, 512), BF16),
+            pltpu.VMEM((128, 128), BF16),
+            *[pltpu.VMEM((1, 128), F32)] * 2,
+            pltpu.VMEM((128, 128), BF16),
             pltpu.VMEM((rows + 2 * STEP, EDGE + cols + 8, 128), F32),
             pltpu.VMEM((4, rows, 128), BF16),
             pltpu.VMEM((2, STEP, cols, 128), BF16),
@@ -285,7 +338,8 @@
             pltpu.VMEM((n, group, rows // 2, 128), BF16),
             pltpu.VMEM((n, group, rows // 2, 128), BF16),
             pltpu.VMEM((rows, cols, 128), F32),
-            dma((8,)), dma((8,)), dma((n,)), dma((n,)), dma((n,)), dma((n,)),
+            dma((10,)), dma((8,)), dma((8,)), dma((n,)), dma((n,)), dma((n,)), dma((n,)),
+            dma((n_row // 2, n)), dma((n_row // 2, n)),
             dma((n_row,)), dma((n_row,)), dma((n,)), dma((n,)),
         ],
         compiler_params=pltpu.CompilerParams(

time: 33.9 us -> 32.8 us (0.968)
  Pallas kernels: 27.9 us -> 26.8 us
    pallas_call x1, Pallas kernels: 27.9 us -> 26.8 us  [on_device(): pl.pallas_call(functools.partial(kernel, (n_row, n, rows, cols)), out_sha...]
where the time goes in v2:
time: 32.8 us; the launch traced here: 32.5 us
  Pallas kernels  26.8 us (82%)
  local copies, waits for them, and re-layouts  5.64 us (17%)
    pallas_call x1, Pallas kernels, on_device(): pl.pallas_call(functools.partial(kernel, (n_row, n, rows, cols)), out_sha...  26.8 us
    unnamed x21, local copies, waits for them, and re-layouts  5.64 us

profile of v2, /device:TPU:3, one launch (start us, length us, event | category | flops | bytes accessed | tf_op | source)
XLA Modules:
  0.0 32.5 jit_solution(4917355551877727823)
XLA Ops:
  0.0 0.0 copy-start.8
  0.0 0.0 copy-start.9
  0.0 0.0 copy-start.5
  0.0 0.0 copy-start.6
  0.0 0.0 copy-start.7
  0.0 0.6 %copy-done.8 = f32[128]{0:T(128)S(1)} copy-done((f32[128]{0:T(128)S(1)}, f32[128]{0:T(128)}, u32[]{:S(2)}) %copy-start.8) | copy-done | bytes 536
  0.7 0.0 copy-done.9
  0.7 0.0 copy-done.5
  0.7 0.0 copy-done.6
  0.7 0.0 copy-done.7
  0.7 0.0 copy-start
  0.7 1.0 %copy-done = bf16[3,3,128,128]{3,2,1,0:T(8,128)(2,1)S(1)} copy-done((bf16[3,3,128,128]{3,2,1,0:T(8,128)(2,1)S(1)}, bf16[3,3,128,128]{3,2,1,0:T(8,128)(2,1)}, u32[]{:S(2)}) %copy-start) | copy-done | bytes 294936
  1.7 0.0 copy-start.1
  1.7 0.9 %copy-done.1 = bf16[32,16,128]{2,1,0:T(8,128)(2,1)S(1)} copy-done((bf16[32,16,128]{2,1,0:T(8,128)(2,1)S(1)}, bf16[32,16,128]{2,1,0:T(8,128)(2,1)}, u32[]{:S(2)}) %copy-start.1) | copy-done | bytes 131096
  2.6 0.0 copy-start.2
  2.6 0.9 %copy-done.2 = bf16[128,512]{1,0:T(8,128)(2,1)S(1)} copy-done((bf16[128,512]{1,0:T(8,128)(2,1)S(1)}, bf16[128,512]{1,0:T(8,128)(2,1)}, u32[]{:S(2)}) %copy-start.2) | copy-done | bytes 131096
  3.5 0.0 copy-start.3
  3.5 0.8 %copy-done.3 = bf16[128,128]{1,0:T(8,128)(2,1)S(1)} copy-done((bf16[128,128]{1,0:T(8,128)(2,1)S(1)}, bf16[128,128]{1,0:T(8,128)(2,1)}, u32[]{:S(2)}) %copy-start.3) | copy-done | bytes 32792
  4.2 0.0 copy-start.4
  4.3 0.8 %copy-done.4 = bf16[128,128]{1,0:T(8,128)(2,1)S(1)} copy-done((bf16[128,128]{1,0:T(8,128)(2,1)S(1)}, bf16[128,128]{1,0:T(8,128)(2,1)}, u32[]{:S(2)}) %copy-start.4) | copy-done | bytes 32792
  5.0 26.8 %shard_map.100 = bf16[32,16,128]{2,1,0:T(8,128)(2,1)S(1)} custom-call(bf16[32,16,128]{2,1,0:T(8,128)(2,1)S(1)} %copy-done.1, bf16[3,384,128]{2,1,0:T(8,128)(2,1)S(1)} %bitcast.6, f32[1,128]{1,0:T(1,128)S(1)} %bitcast.7, f32[1,128]{1,0:T(1,128)S(1)} %bitcast.8, f32[1,128]{1,0:T(1,128)S(1)} %bitcast.9, bf16[128,512]{1,0:T(8,128)(2,1)S(1)} %copy-done.2, ...), custom_call_target="tpu_custom_call" | custom-call | tf_op jit(solution)/shard_map/pallas_call | solution.py:312
  31.8 0.7 %copy.12 = bf16[32,16,128]{2,1,0:T(8,128)(2,1)} copy(bf16[32,16,128]{2,1,0:T(8,128)(2,1)S(1)} %shard_map.100) | data formatting | bytes 262144
Async XLA Ops:
  0.0 0.7 %copy-start.8 = (f32[128]{0:T(128)S(1)}, f32[128]{0:T(128)}, u32[]{:S(2)}) copy-start(f32[128]{0:T(128)} %param.17) | copy-start | bytes 1540
  0.0 0.7 %copy-start.9 = (f32[128]{0:T(128)S(1)}, f32[128]{0:T(128)}, u32[]{:S(2)}) copy-start(f32[128]{0:T(128)} %param.18) | copy-start | bytes 1540
  0.0 0.7 %copy-start.5 = (f32[128]{0:T(128)S(1)}, f32[128]{0:T(128)}, u32[]{:S(2)}) copy-start(f32[128]{0:T(128)} %param.12) | copy-start | bytes 1540
  0.0 0.7 %copy-start.6 = (f32[128]{0:T(128)S(1)}, f32[128]{0:T(128)}, u32[]{:S(2)}) copy-start(f32[128]{0:T(128)} %param.13) | copy-start | bytes 1540
  0.0 0.7 %copy-start.7 = (f32[128]{0:T(128)S(1)}, f32[128]{0:T(128)}, u32[]{:S(2)}) copy-start(f32[128]{0:T(128)} %param.14) | copy-start | bytes 1540
  0.7 1.0 %copy-start = (bf16[3,3,128,128]{3,2,1,0:T(8,128)(2,1)S(1)}, bf16[3,3,128,128]{3,2,1,0:T(8,128)(2,1)}, u32[]{:S(2)}) copy-start(bf16[3,3,128,128]{3,2,1,0:T(8,128)(2,1)} %param.11) | copy-start | bytes 884740
  1.7 0.9 %copy-start.1 = (bf16[32,16,128]{2,1,0:T(8,128)(2,1)S(1)}, bf16[32,16,128]{2,1,0:T(8,128)(2,1)}, u32[]{:S(2)}) copy-start(bf16[32,16,128]{2,1,0:T(8,128)(2,1)} %pair_in.1) | copy-start | bytes 393220
  2.6 0.9 %copy-start.2 = (bf16[128,512]{1,0:T(8,128)(2,1)S(1)}, bf16[128,512]{1,0:T(8,128)(2,1)}, u32[]{:S(2)}) copy-start(bf16[128,512]{1,0:T(8,128)(2,1)} %proj_w_in.1) | copy-start | bytes 393220
  3.5 0.8 %copy-start.3 = (bf16[128,128]{1,0:T(8,128)(2,1)S(1)}, bf16[128,128]{1,0:T(8,128)(2,1)}, u32[]{:S(2)}) copy-start(bf16[128,128]{1,0:T(8,128)(2,1)} %gate_w_in.1) | copy-start | bytes 98308
  4.2 0.8 %copy-start.4 = (bf16[128,128]{1,0:T(8,128)(2,1)S(1)}, bf16[128,128]{1,0:T(8,128)(2,1)}, u32[]{:S(2)}) copy-start(bf16[128,128]{1,0:T(8,128)(2,1)} %out_w_in.1) | copy-start | bytes 98308
